TPU v7x, 256 devices: a whole 4x4x8 slice. The times are simulated.
256 devices in a mesh: space: 16 (over y, z_lo, core), rot: 16 (over z_hi, x).
Axes of the slice: x: 4, y: 4, z: 8 (z_hi: 4, z_lo: 2; z = z_hi * 2 + z_lo), core: 2. Of those that a mesh axis runs over, the one named last changes fastest.
Arguments:
- tomogram: float32 [256, 6144], P('space'), may hold values from -6 to 6
- templates: bfloat16 [64, 32768], P('space'), may hold values from -6 to 6
- rot_ids: int32 [16], P('rot'), may hold values from 0 to 63
Outputs:
- best_score: float32 [256, 6144], P('space', 'rot')
- score_mass: float32 [256, 6144], P('space', 'rot')
Inputs may be any that keep to these rules, and one draw needn't show every extreme that they name: `rot_ids`: each entry names a template of the bank.
All inputs are finite; a program needn't handle non-finite values.
Results may differ from a plain program's by a relative error of at most 0.0003.
Values may be sent and summed in bfloat16 or wider, within the bound.
No kernel may reach another device: no remote copies, remote signals or barrier semaphores. Data moves between devices by JAX's collectives and lax.ppermute only.
A program may use at most 64 MiB of HBM per device.

v0:
```python
import functools
import math

import jax
import jax.numpy as jnp
import numpy as np
from jax import lax
from jax.experimental import pallas as pl
from jax.experimental.pallas import tpu as pltpu
from jax.sharding import PartitionSpec as P

NY = 64
NZ = 96
TS = 32
HALF = TS // 2
LY = NY + HALF
LZ = NZ + HALF
KZ = LZ // 2 + 1
LANES = 128
MID = LANES // 2

sharpness = 0.4
SENT = 256.0
SCALE = 8192.0
ROT_X = 4
SEND_ORDER = list(range(15, -1, -1))


def angles(length, rows, columns):
    return (np.outer(rows, columns) % length) * (2.0 * math.pi / length)


def halves(table):
    high = np.asarray(table, np.float32).astype(jnp.bfloat16)
    low = (np.asarray(table, np.float64) - high.astype(np.float64)).astype(jnp.bfloat16)
    return high, low


def forward_z(first, count):
    turn = angles(LZ, np.arange(count) + first, np.arange(KZ))
    table = np.zeros((count, LANES))
    table[:, :KZ] = np.cos(turn)
    table[:, MID : MID + KZ] = -np.sin(turn)
    return table


def forward_y(positions):
    turn = angles(LY, np.arange(LY), positions)
    return np.concatenate([np.cos(turn), np.sin(turn)], axis=0)


def inverse_y(order):
    turn = angles(LY, order, np.arange(LY))
    return np.concatenate([np.cos(turn), np.sin(turn)], axis=0)


def inverse_z():
    turn = angles(LZ, np.arange(KZ), np.arange(NZ))
    weight = np.where((np.arange(KZ) == 0) | (np.arange(KZ) == LZ // 2), 1.0, 2.0) / (LY * LZ)
    table = np.zeros((LANES, NZ))
    table[:KZ] = np.cos(turn) * weight[:, None]
    table[MID : MID + KZ] = -np.sin(turn) * weight[:, None]
    return table


def band(count):
    offset = np.arange(count)[:, None] + HALF - np.arange(count)[None, :]
    return ((offset >= 0) & (offset < TS)).astype(np.float64)


def stacked_left(table):
    high, low = halves(table)
    return np.concatenate([high, high, low], axis=1)


def wide_right(table):
    high, low = halves(table)
    rows = np.zeros((LANES - table.shape[0], 2 * table.shape[1]), high.dtype)
    first = np.concatenate([high, low], axis=1)
    second = np.concatenate([high, np.zeros_like(high)], axis=1)
    return np.concatenate([first, rows, second, rows], axis=0)


def split(values):
    high = values.astype(jnp.bfloat16)
    low = (values - high.astype(jnp.float32)).astype(jnp.bfloat16)
    return high, low


def dot(left, right):
    return jnp.dot(left, right, preferred_element_type=jnp.float32)


def dot_right(values, high_table, low_table):
    high, low = split(values)
    return dot(high, high_table) + dot(low, high_table) + dot(high, low_table)


def dot_wide(values, table):
    high, low = split(values)
    blank = [jnp.zeros((values.shape[0], LANES - values.shape[1]), jnp.bfloat16)] if values.shape[1] < LANES else []
    both = dot(jnp.concatenate([high, *blank, low, *blank], axis=1), table)
    return both[:, : both.shape[1] // 2] + both[:, both.shape[1] // 2 :]


def dot_left(stack, values):
    high, low = split(values)
    return dot(stack, jnp.concatenate([high, low, high], axis=0))


def lane_block(tile, part, parts):
    width = tile.shape[1] // parts
    lane = lax.broadcasted_iota(jnp.int32, (1, tile.shape[1]), 1)
    keep = (lane >= part * width) & (lane < (part + 1) * width)
    return tile * keep.astype(jnp.float32).astype(jnp.bfloat16)


def row_block(tile, part, parts):
    height = tile.shape[0] // parts
    row = lax.broadcasted_iota(jnp.int32, tile.shape, 0)
    keep = (row >= part * height) & (row < (part + 1) * height)
    return tile * keep.astype(jnp.float32).astype(jnp.bfloat16)


def row_blocks(tile, parts):
    return jnp.concatenate([row_block(tile, part, parts) for part in range(parts)], axis=1)


def sign():
    lane = lax.broadcasted_iota(jnp.int32, (1, LANES), 1)
    return jnp.where(lane < MID, 1.0, -1.0).astype(jnp.float32)


def swapped(values):
    return pltpu.roll(values, MID, 1)


PLANES = 16


def transform(field, spectrum, base, scale, z_wide, y_table):
    flip = sign()

    def planes(step, carry):
        start = step * PLANES
        block = field[pl.ds(start, PLANES)].reshape(PLANES * NY, NZ)
        along_z = dot_wide(block if scale is None else block * scale, z_wide[...])
        for pair in range(0, PLANES, 2):
            two = [along_z[(pair + i) * NY : (pair + i + 1) * NY] for i in range(2)]
            both = dot_left(y_table[...], jnp.concatenate(two, axis=1))
            for i in range(2):
                part = both[:, i * LANES : (i + 1) * LANES]
                spectrum[base + start + pair + i] = part[:LY] + swapped(part[LY:]) * flip
        return carry

    lax.fori_loop(0, field.shape[0] // PLANES, planes, 0)


def volume_kernel(odd, inside, own, near, far, z_wide, y_table, y_band, z_band, spectrum, norm, summed):
    count = own.shape[0]
    is_odd = odd[0] == 1
    low = jnp.where(is_odd, 0, 2 * count)
    scale = inside[0].astype(jnp.float32)
    transform(own, spectrum, count, None, z_wide, y_table)
    transform(near, spectrum, low, None, z_wide, y_table)
    transform(far, spectrum, 2 * count - low, scale, z_wide, y_table)

    for step in range(NY // 8):
        at = pl.ds(step * 8, 8)
        below, above = [], []
        for x in range(count):
            one, two = near[x, at, :], far[x, at, :] * scale
            below.append(jnp.where(is_odd, one, two))
            above.append(jnp.where(is_odd, two, one))
        level = [value * value for value in below + [own[x, at, :] for x in range(count)] + above]
        width = 1
        while width < TS:
            level = [level[x] + level[x + width] for x in range(len(level) - width)]
            width *= 2
        for x in range(count):
            summed[x, at, :] = level[x]

    parts = y_band.shape[0] // count
    along_y = []
    for x in range(count):
        high, low = split(summed[x])
        along_y.append(dot(y_band[...], jnp.concatenate([high, low], axis=0)))
    rows_of = y_band.shape[0] // parts
    total = None
    for part in range(parts):
        piece = [value[part * rows_of : (part + 1) * rows_of] for value in along_y]
        high, low = split(jnp.concatenate(piece, axis=0))
        table = lane_block(z_band[...], part, parts)
        term = dot(high, table) + dot(low, table)
        total = term if total is None else total + term
    norm[...] = 1.0 / (SCALE * jnp.sqrt(total * SCALE**-2 + TS**3 * 1e-06))


def slide(plane, taps, others, count):
    if count <= 2:
        return [
            [functools.reduce(jnp.add, [plane[x + a] * tap for a, tap in enumerate(row)]) for x in range(count)]
            for row in (taps, others)
        ]
    half = count // 2
    need = half + len(taps) // 2 - 1
    even, odd = plane[0::2], plane[1::2]
    first, second = [row[0::2] for row in (taps, others)], [row[1::2] for row in (taps, others)]
    added = [[one + two for one, two in zip(*pair)] for pair in zip(first, second)]
    shared = slide(odd[:need], *added, half)
    low = slide([even[i] - odd[i] for i in range(need)], *first, half)
    high = slide([even[i + 1] - odd[i] for i in range(need)], *second, half)
    return [[shared[r][x // 2] + (high if x % 2 else low)[r][x // 2] for x in range(count)] for r in range(2)]


def template_kernel(
    apart, odd, held, four, eight, twelve, spectrum, norm, z_high, z_low, y_table, back_y, back_high, back_low, scores, same, cross, product
):
    flip = sign()
    first = flip > 0
    values = held[...].astype(jnp.float32)
    for step, other in ((4, four), (8, eight), (12, twelve)):
        values = jnp.where(apart[0] == step, other[...].astype(jnp.float32), values)
    size = values.shape[0] * values.shape[1]
    centred = values - jnp.sum(values) / size
    scale = 1.0 / jnp.sqrt(jnp.full((1, 1), jnp.sum(centred * centred) / size) + 1e-06)
    groups = values.shape[1] // TS
    along_z = dot_right(centred, row_blocks(z_high[...], groups), row_blocks(z_low[...], groups))
    deep = TS // groups

    def tap(a):
        rows = along_z[a * deep : (a + 1) * deep]
        return jnp.concatenate([rows[:, j * LANES : (j + 1) * LANES] for j in range(groups)], axis=0)

    for a in range(0, TS, 2):
        both = dot_left(y_table[...], jnp.concatenate([tap(a), tap(a + 1)], axis=1))
        for i in range(2):
            part = both[:, i * LANES : (i + 1) * LANES]
            value = part[:LY] + swapped(part[LY:]) * flip
            turned = swapped(value)
            same[a + i] = jnp.where(first, value, turned)
            cross[a + i] = jnp.where(first, -turned, value)

    out = spectrum.shape[0] - TS

    def rows(step, carry):
        at = pl.ds(pl.multiple_of(step * 8, 8), 8)
        plane = [spectrum[x, at, :] for x in range(out + TS)]
        taps, others = [[table[a, at, :] for a in range(TS)] for table in (same, cross)]
        straight, turned = slide(plane, taps, others, out)
        for x in range(out):
            product[x, at, :] = straight[x] + swapped(turned[x])
        return carry

    lax.fori_loop(0, LY // 8, rows, 0)

    fields = []
    for x in range(0, out, 2):
        both = dot_left(back_y[...], jnp.concatenate([product[x], product[x + 1]], axis=1))
        for i in range(2):
            part = both[:, i * LANES : (i + 1) * LANES]
            fields.append(part[:NY] - swapped(part[NY:]) * flip)
    parts = norm.shape[1] // NZ
    rows_of = NY // parts
    columns = [
        jnp.concatenate([value[j * rows_of : (j + 1) * rows_of] for value in fields], axis=0) for j in range(parts)
    ]
    result = jnp.concatenate([dot_right(column, back_high[...], back_low[...]) for column in columns], axis=1)
    result = result * (norm[...] * scale)
    for x in range(out):
        for quarter in range(4):
            part = rows_of // 4
            base = (quarter + (1 - 2 * (quarter % 2)) * odd[0]) * part
            scores[pl.ds(base, part), x, :] = result[x * rows_of + quarter * part : x * rows_of + (quarter + 1) * part]


def cost(flops):
    return pl.CostEstimate(flops=flops, bytes_accessed=flops // 1000, transcendentals=0)


PARAMS = pltpu.CompilerParams(vmem_limit_bytes=24 * 2**20)
IN_VMEM = pl.BlockSpec(memory_space=pltpu.VMEM)
IN_SMEM = pl.BlockSpec(memory_space=pltpu.SMEM)


def volume_tables():
    return [wide_right(forward_z(HALF, NZ)), stacked_left(forward_y(np.arange(NY) + HALF))]


def volume_side(odd, inside, own, near, far, parts):
    count = own.shape[0]
    rows_of = NY // parts
    order = np.arange(NY).reshape(rows_of, parts)[SEND_ORDER].T.reshape(-1)
    y_band = band(NY).T[order].astype(jnp.bfloat16)
    tables = volume_tables() + [
        np.concatenate([y_band, y_band], axis=1),
        np.tile(band(NZ), (1, parts)).astype(jnp.bfloat16),
    ]
    return pl.pallas_call(
        volume_kernel,
        out_shape=(
            jax.ShapeDtypeStruct((3 * count, LY, LANES), jnp.float32),
            jax.ShapeDtypeStruct((count * rows_of, parts * NZ), jnp.float32),
        ),
        in_specs=[IN_SMEM, IN_SMEM] + [IN_VMEM] * 7,
        out_specs=(IN_VMEM, IN_VMEM),
        scratch_shapes=[pltpu.VMEM((count, NY, NZ), jnp.float32)],
        compiler_params=PARAMS,
        cost_estimate=cost(10**6),
        name="volume_side",
    )(odd, inside, own, near, far, *[jnp.asarray(table) for table in tables])


def template_side(apart, odd, candidates, spectrum, norm, parts):
    out = spectrum.shape[0] - TS
    rows_of = NY // parts
    groups = LANES // TS
    order = np.arange(NY).reshape(rows_of, parts)[SEND_ORDER].T.reshape(-1)
    taps = np.arange(TS).reshape(TS // groups, groups).T.reshape(-1)
    tables = (
        *halves(np.tile(forward_z(0, TS), (groups, 1))),
        stacked_left(forward_y(taps)),
        stacked_left(inverse_y(order)),
        *halves(inverse_z()),
    )
    return pl.pallas_call(
        template_kernel,
        out_shape=jax.ShapeDtypeStruct((rows_of, out, parts * NZ), jnp.float32),
        in_specs=[IN_SMEM, IN_SMEM] + [IN_VMEM] * 12,
        out_specs=IN_VMEM,
        scratch_shapes=[
            pltpu.VMEM((TS, LY, LANES), jnp.float32),
            pltpu.VMEM((TS, LY, LANES), jnp.float32),
            pltpu.VMEM((out, LY, LANES), jnp.float32),
        ],
        compiler_params=PARAMS,
        cost_estimate=cost(3 * 10**9),
        name="template_side",
    )(apart, odd, *candidates, spectrum, norm, *[jnp.asarray(table) for table in tables])


def join_kernel(scores, best, mass):
    top = scores[0]
    total = jnp.exp(sharpness * top)
    for index in range(1, scores.shape[0]):
        value = scores[index]
        top = jnp.maximum(top, value)
        total = total + jnp.exp(sharpness * value)
    best[...] = top
    mass[...] = jnp.log(total) / sharpness


def join(scores):
    shape = jax.ShapeDtypeStruct(scores.shape[1:], jnp.float32)
    return pl.pallas_call(
        join_kernel,
        out_shape=(shape, shape),
        in_specs=[IN_VMEM],
        out_specs=(IN_VMEM, IN_VMEM),
        compiler_params=PARAMS,
        name="join",
    )(scores)


def exchange(value, step):
    return lax.ppermute(value, "space", [(i, i ^ step) for i in range(lax.axis_size("space"))])


def next_slab(slab):
    count, copies = lax.axis_size("space"), lax.axis_size("rot")
    pairs = []
    for first in range(1, count, 2):
        ahead = ROT_X if first % 4 == 3 else 0
        for copy in range(copies):
            one = first * copies + copy
            two = (first + 1) % count * copies + (copy + ahead) % copies
            pairs += [(one, two), (two, one)]
    return lax.ppermute(slab, ("space", "rot"), pairs)


def send_groups():
    size = len(SEND_ORDER) // 4
    groups = []
    for slab in range(lax.axis_size("space")):
        quarters = [SEND_ORDER[(place ^ (slab & 1)) * size :][:size] for place in range(4)]
        groups.append([slab * len(SEND_ORDER) + copy for quarter in quarters for copy in quarter])
    return groups


def shards(tomogram, templates, rot_ids):
    parts = lax.axis_size("rot")
    me = lax.axis_index("space")
    bank = templates.shape[0]
    wanted = rot_ids[0]
    apart = me ^ lax.div(wanted, bank)
    held = lax.dynamic_slice(templates, (lax.rem(wanted, bank), 0), (1, templates.shape[1])).reshape(-1)
    scaled = tomogram * SCALE
    sent = scaled.astype(jnp.float16)
    held = jnp.where((apart & 1) == 0, held, exchange(held, 1))
    held, sent, scaled = lax.optimization_barrier((held, sent, scaled))
    near = exchange(scaled, 1).reshape(-1, NY, NZ)
    own = scaled.reshape(-1, NY, NZ)
    far = next_slab(sent)
    held = jnp.where((apart & 2) == 0, held, exchange(held, 2))
    held, near, own = lax.optimization_barrier((held, near, own))
    others = [exchange(held, step) for step in (4, 8, 12)]
    candidates = [value.reshape(-1, LANES) for value in (held, *others)]
    far = far.astype(jnp.float32).reshape(-1, NY, NZ)
    inside = ((me > 0) & (me < lax.axis_size("space") - 1)).astype(jnp.int32).reshape(1)
    spectrum, norm = volume_side((me & 1).reshape(1), inside, own, near, far, NY // parts)
    blocks = template_side((apart & 12).reshape(1), (me & 1).reshape(1), candidates, spectrum, norm, NY // parts)
    arrived = lax.all_to_all((blocks * SENT).astype(jnp.float16), ("space", "rot"), 0, 0, axis_index_groups=send_groups())
    return join(arrived.astype(jnp.float32) * (1.0 / SENT))


def solution(mesh):
    return jax.shard_map(
        shards,
        mesh=mesh,
        in_specs=(P("space", None), P("space", None), P("rot")),
        out_specs=(P("space", "rot"), P("space", "rot")),
        check_vma=False,
    )
```

profile of v0, /device:TPU:38, one launch (start us, length us, event | category | flops | bytes accessed | tf_op | source)
XLA Modules:
  0.0 40.9 jit_solution(17536831036958124976)
XLA Ops:
  0.6 0.0 copy-start
  1.3 0.3 copy-done
  1.6 0.4 dynamic-slice_reduce_fusion
  2.0 0.1 collective-permute-start
  2.1 1.0 %broadcast_multiply_fusion = (f32[16,6144]{1,0:T(8,128)S(1)}, f16[16,6144]{1,0:T(8,128)(2,1)S(1)}) fusion(f32[16,6144]{1,0:T(8,128)} %param.13), kind=kLoop, calls=%fused_computation.2 | loop fusion | flops 196608 | bytes 983040 | tf_op jit(solution)/shard_map/mul | solution.py:397
  3.1 0.0 copy-start.1
  3.1 0.0 copy-start.2
  3.2 0.0 copy-start.3
  3.2 0.0 copy-start.4
  3.2 0.1 collective-permute-done
  3.3 0.2 collective-permute-start.1
  3.6 0.4 collective-permute-start.2
  3.9 0.2 reshape.46.own
  4.1 1.8 %collective-permute-start.6 = (f16[16,6144]{1,0:T(8,128)(2,1)S(1)}, f16[16,6144]{1,0:T(8,128)(2,1)S(1)}, u32[]{:S(2)}, u32[]{:S(2)}) collective-permute-start(f16[16,6144]{1,0:T(8,128)(2,1)S(1)} %get-tuple-element.15), channel_id=1, source_target_pairs={{16,32},{32,16},{17,33},{33,17},{18,34},{34,18},{19,35},{35,19},{2... | collective-permute-start | bytes 589832 | tf_op jit(solution)/shard_map/ppermute | solution.py:378
  5.9 2.5 %collective-permute-done.1 = bf16[32768]{0:T(1024)(128)(2,1)S(1)} collective-permute-done((bf16[32768]{0:T(1024)(128)(2,1)S(1)}, bf16[32768]{0:T(1024)(128)(2,1)S(1)}, u32[]{:S(2)}, u32[]{:S(2)}) %collective-permute-start.1) | collective-permute-done | bytes 65568 | tf_op jit(solution)/shard_map/ppermute | solution.py:366
  8.4 0.0 copy-start.5
  8.4 0.0 copy-start.6
  8.4 0.0 copy-start.7
  8.4 0.0 copy-start.8
  8.4 0.0 copy-start.9
  8.4 0.0 copy-start.10
  8.4 0.0 collective-permute-done.2
  8.5 0.2 reshape.45.near
  8.7 1.7 %collective-permute-start.3 = (bf16[32768]{0:T(1024)(128)(2,1)S(1)}, bf16[32768]{0:T(1024)(128)(2,1)S(1)}, u32[]{:S(2)}, u32[]{:S(2)}) collective-permute-start(bf16[32768]{0:T(1024)(128)(2,1)S(1)} %broadcast_select_fusion.1), channel_id=1, source_target_pairs={{0,64},{16,80},{32,96},{48,112},{64,0},{80,16},{96,32},{112,48},{1... | collective-permute-start | bytes 196616 | tf_op jit(solution)/shard_map/ppermute | solution.py:366
  10.3 2.9 %collective-permute-start.4 = (bf16[32768]{0:T(1024)(128)(2,1)S(1)}, bf16[32768]{0:T(1024)(128)(2,1)S(1)}, u32[]{:S(2)}, u32[]{:S(2)}) collective-permute-start(bf16[32768]{0:T(1024)(128)(2,1)S(1)} %broadcast_select_fusion.1), channel_id=1, source_target_pairs={{0,128},{16,144},{32,160},{48,176},{64,192},{80,208},{96,224},{112... | collective-permute-start | bytes 196616 | tf_op jit(solution)/shard_map/ppermute | solution.py:366
  13.2 0.2 collective-permute-start.5
  13.4 0.0 collective-permute-done.6
  13.5 0.2 reshape.58.far
  13.7 0.0 copy-done.1
  13.7 0.0 copy-done.2
  13.7 0.0 copy-done.3
  13.7 0.0 copy-done.4
  13.7 2.8 %volume_side.1 = (f32[48,80,128]{2,1,0:T(8,128)S(1)}, f32[256,384]{1,0:T(8,128)S(1)}) custom-call(s32[1]{0:T(128)} %bitcast.2.odd, s32[1]{0:T(128)} %bitcast.7.inside, f32[16,64,96]{2,1,0:T(8,128)S(1)} %reshape.46.own, f32[16,64,96]{2,1,0:T(8,128)S(1)} %reshape.45.near, f32[16,64,96]{2,1,0:T(8,128)S(1)} %reshape.58.far, bf16[256,256]{1,0:T(8,128)(2,1)S(1)} %copy-done.1, ...), custom_call_target="tpu_custom_call" | custom-call | flops 1000000 | bytes 1000 | tf_op jit(solution)/shard_map/volume_side/pallas_call | solution.py:299
  16.5 0.0 collective-permute-done.3
  16.5 0.3 collective-permute-done.4
  16.8 1.9 %collective-permute-done.5 = bf16[32768]{0:T(1024)(128)(2,1)S(1)} collective-permute-done((bf16[32768]{0:T(1024)(128)(2,1)S(1)}, bf16[32768]{0:T(1024)(128)(2,1)S(1)}, u32[]{:S(2)}, u32[]{:S(2)}) %collective-permute-start.5) | collective-permute-done | bytes 65568 | tf_op jit(solution)/shard_map/ppermute | solution.py:366
  18.7 0.0 copy-done.5
  18.7 0.0 copy-done.6
  18.7 0.0 copy-done.7
  18.7 0.0 copy-done.8
  18.7 0.0 copy-done.9
  18.7 0.0 copy-done.10
  18.7 4.5 %template_side.1 = f32[16,16,384]{2,1,0:T(8,128)S(1)} custom-call(s32[1]{0:T(128)} %bitcast.1.apart, s32[1]{0:T(128)} %bitcast.2.odd, bf16[256,128]{1,0:T(8,128)(2,1)S(1)} %bitcast.11, bf16[256,128]{1,0:T(8,128)(2,1)S(1)} %bitcast.12, bf16[256,128]{1,0:T(8,128)(2,1)S(1)} %bitcast.13, bf16[256,128]{1,0:T(8,128)(2,1)S(1)} %bitcast.14, ...), custom_call_target="tpu_custom_call" | custom-call | flops 3000000000 | bytes 3000000 | tf_op jit(solution)/shard_map/template_side/pallas_call | solution.py:326
  23.3 16.9 %all_to_all.5 = f16[16,16,384]{2,1,0:T(8,128)(2,1)S(1)} all-to-all(f16[16,16,384]{2,1,0:T(8,128)(2,1)S(1)} %multiply_convert_fusion), channel_id=1, replica_groups={{15,14,13,12,11,10,9,8,7,6,5,4,3,2,1,0},{27,26,25,24,31,30,29,28,19,18,..., dimensions={0} | all-to-all | bytes 393216 | tf_op jit(solution)/shard_map/all_to_all | solution.py:412
  40.2 0.7 %join.1 = (f32[16,384]{1,0:T(8,128)}, f32[16,384]{1,0:T(8,128)}) custom-call(f32[16,16,384]{2,1,0:T(8,128)S(1)} %convert_multiply_fusion.scores), custom_call_target="tpu_custom_call" | custom-call | tf_op jit(solution)/shard_map/join/pallas_call | solution.py:355
  (5 shorter events, 0.1 us)
Async XLA Ops:
  0.6 1.0 %copy-start = (bf16[4,32768]{1,0:T(4,128)(2,1)S(1)}, bf16[4,32768]{1,0:T(4,128)(2,1)}, u32[]{:S(2)}) copy-start(bf16[4,32768]{1,0:T(4,128)(2,1)} %param.14) | copy-start | bytes 786436
  2.0 1.3 %collective-permute-start = (bf16[32768]{0:T(1024)(128)(2,1)S(1)}, bf16[32768]{0:T(1024)(128)(2,1)S(1)}, u32[]{:S(2)}, u32[]{:S(2)}) collective-permute-start(bf16[32768]{0:T(1024)(128)(2,1)S(1)} %dynamic-slice_reduce_fusion), channel_id=1, source_target_pairs={{0,16},{16,0},{32,48},{48,32},{64,80},{80,64},{96,112},{112,96},{1... | collective-permute-start | bytes 196616 | tf_op jit(solution)/shard_map/ppermute | solution.py:366
  3.1 10.5 %copy-start.1 = (bf16[256,256]{1,0:T(8,128)(2,1)S(1)}, bf16[256,256]{1,0:T(8,128)(2,1)}, u32[]{:S(2)}) copy-start(bf16[256,256]{1,0:T(8,128)(2,1)} %constant.48.clone.z_wide) | copy-start | bytes 393220
  3.1 10.5 %copy-start.2 = (bf16[160,192]{1,0:T(8,128)(2,1)S(1)}, bf16[160,192]{1,0:T(8,128)(2,1)}, u32[]{:S(2)}) copy-start(bf16[160,192]{1,0:T(8,128)(2,1)} %constant.49.clone.y_table) | copy-start | bytes 184324
  3.2 10.5 %copy-start.3 = (bf16[96,384]{1,0:T(8,128)(2,1)S(1)}, bf16[96,384]{1,0:T(8,128)(2,1)}, u32[]{:S(2)}) copy-start(bf16[96,384]{1,0:T(8,128)(2,1)} %constant.51.clone.z_band) | copy-start | bytes 221188
  3.2 10.5 %copy-start.4 = (bf16[64,128]{1,0:T(8,128)(2,1)S(1)}, bf16[64,128]{1,0:T(8,128)(2,1)}, u32[]{:S(2)}) copy-start(bf16[64,128]{1,0:T(8,128)(2,1)} %constant.50.clone.y_band) | copy-start | bytes 49156
  3.3 5.0 %collective-permute-start.1 = (bf16[32768]{0:T(1024)(128)(2,1)S(1)}, bf16[32768]{0:T(1024)(128)(2,1)S(1)}, u32[]{:S(2)}, u32[]{:S(2)}) collective-permute-start(bf16[32768]{0:T(1024)(128)(2,1)S(1)} %broadcast_select_fusion), channel_id=1, source_target_pairs={{0,32},{16,48},{32,0},{48,16},{64,96},{80,112},{96,64},{112,80},{1... | collective-permute-start | bytes 196616 | tf_op jit(solution)/shard_map/ppermute | solution.py:366
  3.6 4.9 %collective-permute-start.2 = (f32[16,6144]{1,0:T(8,128)S(1)}, f32[16,6144]{1,0:T(8,128)S(1)}, u32[]{:S(2)}, u32[]{:S(2)}) collective-permute-start(f32[16,6144]{1,0:T(8,128)S(1)} %get-tuple-element.11), channel_id=1, source_target_pairs={{0,16},{16,0},{32,48},{48,32},{64,80},{80,64},{96,112},{112,96},{1... | collective-permute-start | bytes 1179656 | tf_op jit(solution)/shard_map/ppermute | solution.py:366
  4.1 9.3 %collective-permute-start.6 = (f16[16,6144]{1,0:T(8,128)(2,1)S(1)}, f16[16,6144]{1,0:T(8,128)(2,1)S(1)}, u32[]{:S(2)}, u32[]{:S(2)}) collective-permute-start(f16[16,6144]{1,0:T(8,128)(2,1)S(1)} %get-tuple-element.15), channel_id=1, source_target_pairs={{16,32},{32,16},{17,33},{33,17},{18,34},{34,18},{19,35},{35,19},{2... | collective-permute-start | bytes 589832 | tf_op jit(solution)/shard_map/ppermute | solution.py:378
  8.4 10.3 %copy-start.5 = (bf16[128,240]{1,0:T(8,128)(2,1)S(1)}, bf16[128,240]{1,0:T(8,128)(2,1)}, u32[]{:S(2)}) copy-start(bf16[128,240]{1,0:T(8,128)(2,1)} %constant.55.clone.back_y) | copy-start | bytes 184324
  8.4 10.3 %copy-start.6 = (bf16[160,96]{1,0:T(8,128)(2,1)S(1)}, bf16[160,96]{1,0:T(8,128)(2,1)}, u32[]{:S(2)}) copy-start(bf16[160,96]{1,0:T(8,128)(2,1)} %constant.54.clone.y_table) | copy-start | bytes 92164
  8.4 10.3 %copy-start.7 = (bf16[128,128]{1,0:T(8,128)(2,1)S(1)}, bf16[128,128]{1,0:T(8,128)(2,1)}, u32[]{:S(2)}) copy-start(bf16[128,128]{1,0:T(8,128)(2,1)} %constant.52.clone.z_high) | copy-start | bytes 98308
  8.4 10.3 %copy-start.8 = (bf16[128,128]{1,0:T(8,128)(2,1)S(1)}, bf16[128,128]{1,0:T(8,128)(2,1)}, u32[]{:S(2)}) copy-start(bf16[128,128]{1,0:T(8,128)(2,1)} %constant.53.clone.z_low) | copy-start | bytes 98308
  8.4 10.3 %copy-start.9 = (bf16[128,96]{1,0:T(8,128)(2,1)S(1)}, bf16[128,96]{1,0:T(8,128)(2,1)}, u32[]{:S(2)}) copy-start(bf16[128,96]{1,0:T(8,128)(2,1)} %constant.56.clone.back_high) | copy-start | bytes 73732
  8.4 10.3 %copy-start.10 = (bf16[128,96]{1,0:T(8,128)(2,1)S(1)}, bf16[128,96]{1,0:T(8,128)(2,1)}, u32[]{:S(2)}) copy-start(bf16[128,96]{1,0:T(8,128)(2,1)} %constant.57.clone.back_low) | copy-start | bytes 73732
  8.7 7.8 %collective-permute-start.3 = (bf16[32768]{0:T(1024)(128)(2,1)S(1)}, bf16[32768]{0:T(1024)(128)(2,1)S(1)}, u32[]{:S(2)}, u32[]{:S(2)}) collective-permute-start(bf16[32768]{0:T(1024)(128)(2,1)S(1)} %broadcast_select_fusion.1), channel_id=1, source_target_pairs={{0,64},{16,80},{32,96},{48,112},{64,0},{80,16},{96,32},{112,48},{1... | collective-permute-start | bytes 196616 | tf_op jit(solution)/shard_map/ppermute | solution.py:366
  10.3 6.5 %collective-permute-start.4 = (bf16[32768]{0:T(1024)(128)(2,1)S(1)}, bf16[32768]{0:T(1024)(128)(2,1)S(1)}, u32[]{:S(2)}, u32[]{:S(2)}) collective-permute-start(bf16[32768]{0:T(1024)(128)(2,1)S(1)} %broadcast_select_fusion.1), channel_id=1, source_target_pairs={{0,128},{16,144},{32,160},{48,176},{64,192},{80,208},{96,224},{112... | collective-permute-start | bytes 196616 | tf_op jit(solution)/shard_map/ppermute | solution.py:366
  13.2 5.5 %collective-permute-start.5 = (bf16[32768]{0:T(1024)(128)(2,1)S(1)}, bf16[32768]{0:T(1024)(128)(2,1)S(1)}, u32[]{:S(2)}, u32[]{:S(2)}) collective-permute-start(bf16[32768]{0:T(1024)(128)(2,1)S(1)} %broadcast_select_fusion.1), channel_id=1, source_target_pairs={{0,192},{16,208},{32,224},{48,240},{64,128},{80,144},{96,160},{112... | collective-permute-start | bytes 196616 | tf_op jit(solution)/shard_map/ppermute | solution.py:366
where the time goes:
time: 41.1 us; the launch traced here: 40.9 us
  blocking collectives  16.9 us (41%)
  Pallas kernels  7.95 us (19%)
  starting transfers between devices  7.21 us (18%)
  waiting for transfers between devices  4.83 us (12%)
  between operations  1.59 us (4%)
  local copies, waits for them, and re-layouts  1.29 us (3%)
  other arithmetic  1.16 us (3%)
    all_to_all x1, blocking collectives, shards(): lax.all_to_all((blocks * SENT).astype(jnp.float16), ('space', 'rot'), 0,...  16.9 us
    ppermute x6, starting transfers between devices, exchange(): lax.ppermute(value, 'space', [(i, i ^ step) for i in range(lax.axis_size(...  5.45 us
    ppermute x6, waiting for transfers between devices, exchange(): lax.ppermute(value, 'space', [(i, i ^ step) for i in range(lax.axis_size(...  4.83 us
    pallas_call x1, Pallas kernels, template_side(): pl.pallas_call(template_kernel, out_shape=jax.ShapeDtypeStruct((rows_of,...  4.51 us
    pallas_call x1, Pallas kernels, volume_side(): pl.pallas_call(volume_kernel, out_shape=(jax.ShapeDtypeStruct((3 * count,...  2.75 us
    ppermute x1, starting transfers between devices, next_slab(): return lax.ppermute(slab, ('space', 'rot'), pairs)  1.76 us
    mul x1, other arithmetic, shards(): scaled = tomogram * SCALE  1.04 us
  transfers between devices with their start and end apart: 7, of which 4 were waited for; matrix products, arithmetic and copies ran while one was open for 4% of the time, Pallas kernels for 7%

commit v1 on v0

--- a/solution.py
+++ b/solution.py
@@ -398,7 +398,7 @@
     sent = scaled.astype(jnp.float16)
     held = jnp.where((apart & 1) == 0, held, exchange(held, 1))
     held, sent, scaled = lax.optimization_barrier((held, sent, scaled))
-    near = exchange(scaled, 1).reshape(-1, NY, NZ)
+    near = exchange(scaled, 1)
     own = scaled.reshape(-1, NY, NZ)
     far = next_slab(sent)
     held = jnp.where((apart & 2) == 0, held, exchange(held, 2))
@@ -406,6 +406,7 @@
     others = [exchange(held, step) for step in (4, 8, 12)]
     candidates = [value.reshape(-1, LANES) for value in (held, *others)]
     far = far.astype(jnp.float32).reshape(-1, NY, NZ)
+    near = near.reshape(-1, NY, NZ)
     inside = ((me > 0) & (me < lax.axis_size("space") - 1)).astype(jnp.int32).reshape(1)
     spectrum, norm = volume_side((me & 1).reshape(1), inside, own, near, far, NY // parts)
     blocks = template_side((apart & 12).reshape(1), (me & 1).reshape(1), candidates, spectrum, norm, NY // parts)

time: 41.1 us -> 40.9 us (level)
  transfers between devices with their start and end apart: 7 -> 7, of which waited for: 4 -> 3; matrix products, arithmetic and copies ran while one was open for 4% -> 4% of each run, Pallas kernels for 7% -> 7%
where the time goes in v1:
time: 40.9 us; the launch traced here: 40.6 us
  blocking collectives  16.9 us (41%)
  Pallas kernels  7.95 us (19%)
  starting transfers between devices  7.21 us (18%)
  waiting for transfers between devices  4.56 us (11%)
  between operations  1.59 us (4%)
  local copies, waits for them, and re-layouts  1.29 us (3%)
  other arithmetic  1.16 us (3%)
    all_to_all x1, blocking collectives, shards(): lax.all_to_all((blocks * SENT).astype(jnp.float16), ('space', 'rot'), 0,...  16.9 us
    ppermute x6, starting transfers between devices, exchange(): lax.ppermute(value, 'space', [(i, i ^ step) for i in range(lax.axis_size(...  5.45 us
    ppermute x6, waiting for transfers between devices, exchange(): lax.ppermute(value, 'space', [(i, i ^ step) for i in range(lax.axis_size(...  4.56 us
    pallas_call x1, Pallas kernels, template_side(): pl.pallas_call(template_kernel, out_shape=jax.ShapeDtypeStruct((rows_of,...  4.51 us
    pallas_call x1, Pallas kernels, volume_side(): pl.pallas_call(volume_kernel, out_shape=(jax.ShapeDtypeStruct((3 * count,...  2.75 us
    ppermute x1, starting transfers between devices, next_slab(): return lax.ppermute(slab, ('space', 'rot'), pairs)  1.76 us
    mul x1, other arithmetic, shards(): scaled = tomogram * SCALE  1.04 us
  transfers between devices with their start and end apart: 7, of which 3 were waited for; matrix products, arithmetic and copies ran while one was open for 4% of the time, Pallas kernels for 7%

profile of v1, /device:TPU:38, one launch (start us, length us, event | category | flops | bytes accessed | tf_op | source)
XLA Modules:
  0.0 40.6 jit_solution(6160852085930244748)
XLA Ops:
  0.6 0.0 copy-start
  1.3 0.3 copy-done
  1.6 0.4 dynamic-slice_reduce_fusion
  2.0 0.1 collective-permute-start
  2.1 1.0 %broadcast_multiply_fusion = (f32[16,6144]{1,0:T(8,128)S(1)}, f16[16,6144]{1,0:T(8,128)(2,1)S(1)}) fusion(f32[16,6144]{1,0:T(8,128)} %param.13), kind=kLoop, calls=%fused_computation.2 | loop fusion | flops 196608 | bytes 983040 | tf_op jit(solution)/shard_map/mul | solution.py:397
  3.1 0.0 copy-start.1
  3.1 0.0 copy-start.2
  3.2 0.0 copy-start.3
  3.2 0.0 copy-start.4
  3.2 0.1 collective-permute-done
  3.3 0.2 collective-permute-start.1
  3.6 0.2 reshape.45.own
  3.8 0.4 collective-permute-start.2
  4.1 1.8 %collective-permute-start.6 = (f16[16,6144]{1,0:T(8,128)(2,1)S(1)}, f16[16,6144]{1,0:T(8,128)(2,1)S(1)}, u32[]{:S(2)}, u32[]{:S(2)}) collective-permute-start(f16[16,6144]{1,0:T(8,128)(2,1)S(1)} %get-tuple-element.15), channel_id=1, source_target_pairs={{16,32},{32,16},{17,33},{33,17},{18,34},{34,18},{19,35},{35,19},{2... | collective-permute-start | bytes 589832 | tf_op jit(solution)/shard_map/ppermute | solution.py:378
  5.9 2.5 %collective-permute-done.1 = bf16[32768]{0:T(1024)(128)(2,1)S(1)} collective-permute-done((bf16[32768]{0:T(1024)(128)(2,1)S(1)}, bf16[32768]{0:T(1024)(128)(2,1)S(1)}, u32[]{:S(2)}, u32[]{:S(2)}) %collective-permute-start.1) | collective-permute-done | bytes 65568 | tf_op jit(solution)/shard_map/ppermute | solution.py:366
  8.4 0.0 collective-permute-done.2
  8.4 1.7 %collective-permute-start.3 = (bf16[32768]{0:T(1024)(128)(2,1)S(1)}, bf16[32768]{0:T(1024)(128)(2,1)S(1)}, u32[]{:S(2)}, u32[]{:S(2)}) collective-permute-start(bf16[32768]{0:T(1024)(128)(2,1)S(1)} %broadcast_select_fusion.1), channel_id=1, source_target_pairs={{0,64},{16,80},{32,96},{48,112},{64,0},{80,16},{96,32},{112,48},{1... | collective-permute-start | bytes 196616 | tf_op jit(solution)/shard_map/ppermute | solution.py:366
  10.0 2.9 %collective-permute-start.4 = (bf16[32768]{0:T(1024)(128)(2,1)S(1)}, bf16[32768]{0:T(1024)(128)(2,1)S(1)}, u32[]{:S(2)}, u32[]{:S(2)}) collective-permute-start(bf16[32768]{0:T(1024)(128)(2,1)S(1)} %broadcast_select_fusion.1), channel_id=1, source_target_pairs={{0,128},{16,144},{32,160},{48,176},{64,192},{80,208},{96,224},{112... | collective-permute-start | bytes 196616 | tf_op jit(solution)/shard_map/ppermute | solution.py:366
  12.9 0.2 collective-permute-start.5
  13.2 0.0 collective-permute-done.6
  13.2 0.0 copy-start.5
  13.2 0.0 copy-start.6
  13.2 0.0 copy-start.7
  13.2 0.0 copy-start.8
  13.2 0.0 copy-start.9
  13.3 0.0 copy-start.10
  13.3 0.2 reshape.58.far
  13.5 0.2 reshape.52.near
  13.7 0.0 copy-done.1
  13.7 0.0 copy-done.2
  13.7 0.0 copy-done.3
  13.7 0.0 copy-done.4
  13.7 2.8 %volume_side.1 = (f32[48,80,128]{2,1,0:T(8,128)S(1)}, f32[256,384]{1,0:T(8,128)S(1)}) custom-call(s32[1]{0:T(128)} %bitcast.2.odd, s32[1]{0:T(128)} %bitcast.7.inside, f32[16,64,96]{2,1,0:T(8,128)S(1)} %reshape.45.own, f32[16,64,96]{2,1,0:T(8,128)S(1)} %reshape.52.near, f32[16,64,96]{2,1,0:T(8,128)S(1)} %reshape.58.far, bf16[256,256]{1,0:T(8,128)(2,1)S(1)} %copy-done.1, ...), custom_call_target="tpu_custom_call" | custom-call | flops 1000000 | bytes 1000 | tf_op jit(solution)/shard_map/volume_side/pallas_call | solution.py:299
  16.5 0.0 collective-permute-done.3
  16.5 0.0 collective-permute-done.4
  16.5 1.9 %collective-permute-done.5 = bf16[32768]{0:T(1024)(128)(2,1)S(1)} collective-permute-done((bf16[32768]{0:T(1024)(128)(2,1)S(1)}, bf16[32768]{0:T(1024)(128)(2,1)S(1)}, u32[]{:S(2)}, u32[]{:S(2)}) %collective-permute-start.5) | collective-permute-done | bytes 65568 | tf_op jit(solution)/shard_map/ppermute | solution.py:366
  18.4 0.0 copy-done.5
  18.4 0.0 copy-done.6
  18.4 0.0 copy-done.7
  18.4 0.0 copy-done.8
  18.4 0.0 copy-done.9
  18.4 0.0 copy-done.10
  18.5 4.5 %template_side.1 = f32[16,16,384]{2,1,0:T(8,128)S(1)} custom-call(s32[1]{0:T(128)} %bitcast.1.apart, s32[1]{0:T(128)} %bitcast.2.odd, bf16[256,128]{1,0:T(8,128)(2,1)S(1)} %bitcast.11, bf16[256,128]{1,0:T(8,128)(2,1)S(1)} %bitcast.12, bf16[256,128]{1,0:T(8,128)(2,1)S(1)} %bitcast.13, bf16[256,128]{1,0:T(8,128)(2,1)S(1)} %bitcast.14, ...), custom_call_target="tpu_custom_call" | custom-call | flops 3000000000 | bytes 3000000 | tf_op jit(solution)/shard_map/template_side/pallas_call | solution.py:326
  23.0 16.9 %all_to_all.5 = f16[16,16,384]{2,1,0:T(8,128)(2,1)S(1)} all-to-all(f16[16,16,384]{2,1,0:T(8,128)(2,1)S(1)} %multiply_convert_fusion), channel_id=1, replica_groups={{15,14,13,12,11,10,9,8,7,6,5,4,3,2,1,0},{27,26,25,24,31,30,29,28,19,18,..., dimensions={0} | all-to-all | bytes 393216 | tf_op jit(solution)/shard_map/all_to_all | solution.py:413
  39.9 0.7 %join.1 = (f32[16,384]{1,0:T(8,128)}, f32[16,384]{1,0:T(8,128)}) custom-call(f32[16,16,384]{2,1,0:T(8,128)S(1)} %convert_multiply_fusion.scores), custom_call_target="tpu_custom_call" | custom-call | tf_op jit(solution)/shard_map/join/pallas_call | solution.py:355
  (5 shorter events, 0.1 us)
Async XLA Ops:
  0.6 1.0 %copy-start = (bf16[4,32768]{1,0:T(4,128)(2,1)S(1)}, bf16[4,32768]{1,0:T(4,128)(2,1)}, u32[]{:S(2)}) copy-start(bf16[4,32768]{1,0:T(4,128)(2,1)} %param.14) | copy-start | bytes 786436
  2.0 1.3 %collective-permute-start = (bf16[32768]{0:T(1024)(128)(2,1)S(1)}, bf16[32768]{0:T(1024)(128)(2,1)S(1)}, u32[]{:S(2)}, u32[]{:S(2)}) collective-permute-start(bf16[32768]{0:T(1024)(128)(2,1)S(1)} %dynamic-slice_reduce_fusion), channel_id=1, source_target_pairs={{0,16},{16,0},{32,48},{48,32},{64,80},{80,64},{96,112},{112,96},{1... | collective-permute-start | bytes 196616 | tf_op jit(solution)/shard_map/ppermute | solution.py:366
  3.1 10.5 %copy-start.1 = (bf16[256,256]{1,0:T(8,128)(2,1)S(1)}, bf16[256,256]{1,0:T(8,128)(2,1)}, u32[]{:S(2)}) copy-start(bf16[256,256]{1,0:T(8,128)(2,1)} %constant.48.clone.z_wide) | copy-start | bytes 393220
  3.1 10.5 %copy-start.2 = (bf16[160,192]{1,0:T(8,128)(2,1)S(1)}, bf16[160,192]{1,0:T(8,128)(2,1)}, u32[]{:S(2)}) copy-start(bf16[160,192]{1,0:T(8,128)(2,1)} %constant.49.clone.y_table) | copy-start | bytes 184324
  3.2 10.5 %copy-start.3 = (bf16[96,384]{1,0:T(8,128)(2,1)S(1)}, bf16[96,384]{1,0:T(8,128)(2,1)}, u32[]{:S(2)}) copy-start(bf16[96,384]{1,0:T(8,128)(2,1)} %constant.51.clone.z_band) | copy-start | bytes 221188
  3.2 10.5 %copy-start.4 = (bf16[64,128]{1,0:T(8,128)(2,1)S(1)}, bf16[64,128]{1,0:T(8,128)(2,1)}, u32[]{:S(2)}) copy-start(bf16[64,128]{1,0:T(8,128)(2,1)} %constant.50.clone.y_band) | copy-start | bytes 49156
  3.3 5.0 %collective-permute-start.1 = (bf16[32768]{0:T(1024)(128)(2,1)S(1)}, bf16[32768]{0:T(1024)(128)(2,1)S(1)}, u32[]{:S(2)}, u32[]{:S(2)}) collective-permute-start(bf16[32768]{0:T(1024)(128)(2,1)S(1)} %broadcast_select_fusion), channel_id=1, source_target_pairs={{0,32},{16,48},{32,0},{48,16},{64,96},{80,112},{96,64},{112,80},{1... | collective-permute-start | bytes 196616 | tf_op jit(solution)/shard_map/ppermute | solution.py:366
  3.8 4.6 %collective-permute-start.2 = (f32[16,6144]{1,0:T(8,128)S(1)}, f32[16,6144]{1,0:T(8,128)S(1)}, u32[]{:S(2)}, u32[]{:S(2)}) collective-permute-start(f32[16,6144]{1,0:T(8,128)S(1)} %get-tuple-element.11), channel_id=1, source_target_pairs={{0,16},{16,0},{32,48},{48,32},{64,80},{80,64},{96,112},{112,96},{1... | collective-permute-start | bytes 1179656 | tf_op jit(solution)/shard_map/ppermute | solution.py:366
  4.1 9.1 %collective-permute-start.6 = (f16[16,6144]{1,0:T(8,128)(2,1)S(1)}, f16[16,6144]{1,0:T(8,128)(2,1)S(1)}, u32[]{:S(2)}, u32[]{:S(2)}) collective-permute-start(f16[16,6144]{1,0:T(8,128)(2,1)S(1)} %get-tuple-element.15), channel_id=1, source_target_pairs={{16,32},{32,16},{17,33},{33,17},{18,34},{34,18},{19,35},{35,19},{2... | collective-permute-start | bytes 589832 | tf_op jit(solution)/shard_map/ppermute | solution.py:378
  8.4 8.1 %collective-permute-start.3 = (bf16[32768]{0:T(1024)(128)(2,1)S(1)}, bf16[32768]{0:T(1024)(128)(2,1)S(1)}, u32[]{:S(2)}, u32[]{:S(2)}) collective-permute-start(bf16[32768]{0:T(1024)(128)(2,1)S(1)} %broadcast_select_fusion.1), channel_id=1, source_target_pairs={{0,64},{16,80},{32,96},{48,112},{64,0},{80,16},{96,32},{112,48},{1... | collective-permute-start | bytes 196616 | tf_op jit(solution)/shard_map/ppermute | solution.py:366
  10.0 6.5 %collective-permute-start.4 = (bf16[32768]{0:T(1024)(128)(2,1)S(1)}, bf16[32768]{0:T(1024)(128)(2,1)S(1)}, u32[]{:S(2)}, u32[]{:S(2)}) collective-permute-start(bf16[32768]{0:T(1024)(128)(2,1)S(1)} %broadcast_select_fusion.1), channel_id=1, source_target_pairs={{0,128},{16,144},{32,160},{48,176},{64,192},{80,208},{96,224},{112... | collective-permute-start | bytes 196616 | tf_op jit(solution)/shard_map/ppermute | solution.py:366
  12.9 5.5 %collective-permute-start.5 = (bf16[32768]{0:T(1024)(128)(2,1)S(1)}, bf16[32768]{0:T(1024)(128)(2,1)S(1)}, u32[]{:S(2)}, u32[]{:S(2)}) collective-permute-start(bf16[32768]{0:T(1024)(128)(2,1)S(1)} %broadcast_select_fusion.1), channel_id=1, source_target_pairs={{0,192},{16,208},{32,224},{48,240},{64,128},{80,144},{96,160},{112... | collective-permute-start | bytes 196616 | tf_op jit(solution)/shard_map/ppermute | solution.py:366
  13.2 5.2 %copy-start.5 = (bf16[128,240]{1,0:T(8,128)(2,1)S(1)}, bf16[128,240]{1,0:T(8,128)(2,1)}, u32[]{:S(2)}) copy-start(bf16[128,240]{1,0:T(8,128)(2,1)} %constant.55.clone.back_y) | copy-start | bytes 184324
  13.2 5.2 %copy-start.6 = (bf16[160,96]{1,0:T(8,128)(2,1)S(1)}, bf16[160,96]{1,0:T(8,128)(2,1)}, u32[]{:S(2)}) copy-start(bf16[160,96]{1,0:T(8,128)(2,1)} %constant.54.clone.y_table) | copy-start | bytes 92164
  13.2 5.2 %copy-start.7 = (bf16[128,128]{1,0:T(8,128)(2,1)S(1)}, bf16[128,128]{1,0:T(8,128)(2,1)}, u32[]{:S(2)}) copy-start(bf16[128,128]{1,0:T(8,128)(2,1)} %constant.52.clone.z_high) | copy-start | bytes 98308
  13.2 5.2 %copy-start.8 = (bf16[128,128]{1,0:T(8,128)(2,1)S(1)}, bf16[128,128]{1,0:T(8,128)(2,1)}, u32[]{:S(2)}) copy-start(bf16[128,128]{1,0:T(8,128)(2,1)} %constant.53.clone.z_low) | copy-start | bytes 98308
  13.2 5.2 %copy-start.9 = (bf16[128,96]{1,0:T(8,128)(2,1)S(1)}, bf16[128,96]{1,0:T(8,128)(2,1)}, u32[]{:S(2)}) copy-start(bf16[128,96]{1,0:T(8,128)(2,1)} %constant.56.clone.back_high) | copy-start | bytes 73732
  13.3 5.2 %copy-start.10 = (bf16[128,96]{1,0:T(8,128)(2,1)S(1)}, bf16[128,96]{1,0:T(8,128)(2,1)}, u32[]{:S(2)}) copy-start(bf16[128,96]{1,0:T(8,128)(2,1)} %constant.57.clone.back_low) | copy-start | bytes 73732
